TPU v7x, 256 devices: a whole 4x4x8 slice. The times are simulated.
256 devices in a mesh: seq: 16 (over z, core), kvh: 4 (over x), rep: 4 (over y).
Axes of the slice: x: 4, y: 4, z: 8, core: 2. Of those that a mesh axis runs over, the one named last changes fastest.
Arguments:
- prompt_kv: bfloat16 [64, 3072, 2048], P('rep', ('seq', 'kvh')), may hold values from -6 to 6
- prompt_len: int32 [64], replicated, may hold values from 1 to 3072, 122880 in all
- request_group: int32 [64], replicated, may hold values from 0 to 63, as said below
- res_kv: bfloat16 [262144, 2048], P(('seq', 'rep'), 'kvh'), may hold values from -6 to 6
- res_len: int32 [64, 31], P(('seq', 'rep')), may hold values from 1 to 2048, 4096 in all within a row
- queries: bfloat16 [2, 2048, 8192], P(None, ('seq', 'rep'), 'kvh'), may hold values from -6.5 to 6.5
- step_kv: bfloat16 [2, 2048, 2048], P(None, ('seq', 'rep'), 'kvh'), may hold values from -6.5 to 6.5
Outputs:
- attention: bfloat16 [2, 2048, 8192], P(None, ('seq', 'rep'), 'kvh')
- landed_cache: bfloat16 [196608, 2048], P(('seq', 'rep'), 'kvh')
Inputs may be any that keep to these rules, and one draw needn't show every extreme that they name: `request_group`: request q lies in prefill group q // 16; its decode group is a seq index times 4 plus a rep index; every decode group receives exactly one request, and at most 4 requests of one prefill group go to one rep index.
All inputs are finite; a program needn't handle non-finite values.
Results may differ from a plain program's by a relative error of at most 0.0049.
Values may be sent and summed in bfloat16 or wider, within the bound.
A program may use at most 128 MiB of HBM per device.

v0:
```python
import jax
import jax.numpy as jnp
from jax import lax
from jax.sharding import PartitionSpec as P

HD = 128
STEPS = 2


def per_device(prompt_kv, prompt_len, request_group, res_kv, res_len, queries, step_kv):
    seq_count = lax.axis_size("seq")
    rep_count = lax.axis_size("rep")
    me_seq = lax.axis_index("seq")
    me_rep = lax.axis_index("rep")
    group_id = me_seq * rep_count + me_rep
    pieces = lax.all_to_all(prompt_kv, "kvh", split_axis=2, concat_axis=1, tiled=True)
    req_count, shard_len, width_dev = pieces.shape
    total_req = request_group.shape[0]
    req_ids = jnp.arange(total_req, dtype=jnp.int32)
    is_mine = request_group == group_id
    own_req = jnp.sum(jnp.where(is_mine, req_ids, 0))
    own_len = jnp.sum(jnp.where(is_mine, prompt_len, 0))
    local_dest = lax.dynamic_slice_in_dim(request_group, me_rep * req_count, req_count)
    local_ids = jnp.arange(req_count, dtype=jnp.int32)
    slot_ids = jnp.arange(seq_count * rep_count, dtype=jnp.int32)
    source = jnp.sum(
        jnp.where(local_dest[None, :] == slot_ids[:, None], local_ids[None, :], 0), axis=1
    )
    outgoing = jnp.take(pieces, source, axis=0)
    arrived = lax.all_to_all(outgoing, ("seq", "rep"), split_axis=0, concat_axis=1, tiled=True)
    arrived = arrived.reshape(seq_count, rep_count, shard_len, width_dev)
    landed = lax.dynamic_index_in_dim(arrived, own_req // req_count, 1, keepdims=False)
    landed = landed.reshape(-1, width_dev)
    positions = jnp.arange(landed.shape[0], dtype=jnp.int32)
    landed = jnp.where((positions < own_len)[:, None], landed, jnp.zeros_like(landed))
    cache_rows = jnp.concatenate([res_kv, landed], axis=0)
    row_count = queries.shape[1]
    res_count = res_kv.shape[0]
    lengths = res_len[0]
    row_ends = jnp.cumsum(lengths)
    starts = row_ends - lengths
    res_pos = jnp.arange(res_count, dtype=jnp.int32)
    member_res = (res_pos[None, :] >= starts[:, None]) & (res_pos[None, :] < row_ends[:, None])
    member_res = jnp.concatenate([member_res, jnp.zeros((1, res_count), bool)], axis=0)
    member_new = jnp.concatenate(
        [jnp.zeros((row_count - 1, landed.shape[0]), bool), (positions < own_len)[None, :]], axis=0
    )
    member = jnp.concatenate([member_res, member_new], axis=1)
    heads_local = width_dev // (2 * HD)
    group_size = queries.shape[2] // (heads_local * HD)
    member_rows = jnp.repeat(member, group_size, axis=0)
    score_scale = HD ** (-0.5)
    step_outputs = []
    for step in range(STEPS):
        per_head = []
        for head in range(heads_local):
            head_keys = cache_rows[:, 2 * head * HD : 2 * head * HD + HD]
            values = cache_rows[:, 2 * head * HD + HD : 2 * (head + 1) * HD]
            query = queries[step, :, head * group_size * HD : (head + 1) * group_size * HD].reshape(
                row_count * group_size, HD
            )
            scores = (
                lax.dot_general(
                    query, head_keys, (((1,), (1,)), ((), ())), preferred_element_type=jnp.float32
                )
                * score_scale
            )
            scores = jnp.where(member_rows, scores, -1e30)
            fresh_k = step_kv[: step + 1, :, 2 * head * HD : 2 * head * HD + HD]
            fresh_v = step_kv[: step + 1, :, 2 * head * HD + HD : 2 * (head + 1) * HD]
            fresh = jnp.einsum(
                "bgd,ubd->bgu",
                query.reshape(row_count, group_size, HD),
                fresh_k,
                preferred_element_type=jnp.float32,
            )
            fresh = fresh.reshape(row_count * group_size, step + 1) * score_scale
            row_max = jnp.maximum(jnp.max(scores, axis=1), jnp.max(fresh, axis=1))
            weight_cache = jnp.exp(scores - row_max[:, None])
            weight_fresh = jnp.exp(fresh - row_max[:, None])
            row_total = jnp.sum(weight_cache, axis=1) + jnp.sum(weight_fresh, axis=1)
            rounded_cache = (weight_cache / row_total[:, None]).astype(jnp.bfloat16)
            rounded_fresh = (weight_fresh / row_total[:, None]).astype(jnp.bfloat16)
            mixed = jnp.dot(rounded_cache, values, preferred_element_type=jnp.float32)
            mixed = mixed + jnp.einsum(
                "bgu,ubd->bgd",
                rounded_fresh.reshape(row_count, group_size, step + 1),
                fresh_v,
                preferred_element_type=jnp.float32,
            ).reshape(row_count * group_size, HD)
            per_head.append(mixed.reshape(row_count, group_size * HD))
        step_outputs.append(jnp.concatenate(per_head, axis=1).astype(jnp.bfloat16))
    attention = jnp.stack(step_outputs)
    return (attention, landed)


def solution(mesh):
    in_specs = (
        P("rep", ("seq", "kvh"), None),
        P(),
        P(),
        P(("seq", "rep"), "kvh"),
        P(("seq", "rep"), None),
        P(None, ("seq", "rep"), "kvh"),
        P(None, ("seq", "rep"), "kvh"),
    )
    out_specs = (P(None, ("seq", "rep"), "kvh"), P(("seq", "rep"), "kvh"))
    return jax.shard_map(
        per_device, mesh=mesh, in_specs=in_specs, out_specs=out_specs, check_vma=False
    )
```

profile of v0, /device:TPU:1, one launch (start us, length us, event | category | flops | bytes accessed | tf_op | source)
XLA Modules:
  0.0 456.5 jit_solution(10555783720233633869)
XLA Ops:
  0.6 10.5 %copy.46 = bf16[16,48,2048]{1,0,2:T(8,128)(2,1)} copy(bf16[16,48,2048]{2,1,0:T(8,128)(2,1)} %param.7) | data formatting | bytes 6291456 | tf_op args[0]
  11.1 14.8 %reshape.386 = bf16[4,2,196608]{2,1,0:T(2,128)(2,1)} reshape(bf16[2048,16,48]{2,1,0:T(8,128)(2,1)} %bitcast.93) | data formatting | bytes 6291456
  25.9 5.0 %all-to-all-start = ((bf16[4,2,196608]{2,1,0:T(2,128)(2,1)}), bf16[4,2,196608]{2,1,0:T(2,128)(2,1)S(1)}, u32[]{:S(2)}, u32[]{:S(2)}) async-start(bf16[4,2,196608]{2,1,0:T(2,128)(2,1)} %reshape.386), calls=%async_computation | async-start | bytes 6291456 | tf_op jit(solution)/shard_map/all_to_all | solution.py:16
  31.0 35.3 %all-to-all-done = bf16[4,2,196608]{2,1,0:T(2,128)(2,1)S(1)} async-done(((bf16[4,2,196608]{2,1,0:T(2,128)(2,1)}), bf16[4,2,196608]{2,1,0:T(2,128)(2,1)S(1)}, u32[]{:S(2)}, u32[]{:S(2)}) %all-to-all-start) | async-done | bytes 3145760 | tf_op jit(solution)/shard_map/all_to_all | solution.py:16
  66.4 9.9 %reshape.387 = bf16[2048,16,48]{2,1,0:T(8,128)(2,1)} reshape(bf16[4,2,196608]{2,1,0:T(2,128)(2,1)S(1)} %all-to-all-done) | data formatting | bytes 6291456
  76.3 10.2 %copy.61 = bf16[16,48,4,512]{3,2,1,0:T(4,128)(2,1)} copy(bf16[16,48,4,512]{1,0,3,2:T(8,128)(2,1)} %bitcast.92) | data formatting | bytes 6291456 | tf_op jit(solution)/shard_map/all_to_all | solution.py:16
  86.5 2.8 copy.48
  89.2 7.0 %gather_fusion = bf16[64,192,512]{2,1,0:T(8,128)(2,1)} fusion(bf16[16,192,512]{2,1,0:T(8,128)(2,1)S(1)} %bitcast.91, s32[1024]{0:T(1024)S(1)} %pad_clamp_fusion), kind=kCustom, calls=%fused_computation | custom fusion | bytes 25166080 | tf_op jit(solution)/shard_map/jit(_take)/gather | solution.py:29
  96.2 10.9 %broadcast_select_fusion = bf16[64,192,512]{2,1,0:T(8,128)(2,1)} fusion(bf16[64,192,512]{2,1,0:T(8,128)(2,1)} %gather_fusion, pred[64]{0:T(512)(128)(4,1)S(1)} %compare_and_fusion), kind=kLoop, calls=%fused_computation.1 | loop fusion | flops 6291456 | bytes 25165888 | tf_op jit(solution)/shard_map/jit(_take)/select_n | solution.py:29
  107.1 14.9 %all-to-all-start.1 = ((bf16[64,192,512]{2,1,0:T(8,128)(2,1)}), bf16[64,192,512]{2,1,0:T(8,128)(2,1)}, u32[]{:S(2)}, u32[]{:S(2)}) async-start(bf16[64,192,512]{2,1,0:T(8,128)(2,1)} %broadcast_select_fusion), calls=%async_computation.1 | async-start | bytes 25165824 | tf_op jit(solution)/shard_map/all_to_all | solution.py:30
  122.1 0.6 fusion.48
  125.6 0.7 iota_compare_fusion.3
  126.3 0.2 fusion.27
  126.5 0.8 broadcast_bitcast_fusion
  127.4 3.3 copy.49
  130.8 0.6 fusion.57
  131.5 0.8 fusion.59
  132.2 0.7 reduce_max.84
  133.0 0.8 fusion.61
  133.7 0.6 reduce_max.80
  134.4 0.6 bitcast_convert_fusion.1
  135.3 0.1 fusion.44
  135.6 0.7 iota_compare_fusion.2
  136.3 257.2 %all-to-all-done.1 = bf16[64,192,512]{2,1,0:T(8,128)(2,1)} async-done(((bf16[64,192,512]{2,1,0:T(8,128)(2,1)}), bf16[64,192,512]{2,1,0:T(8,128)(2,1)}, u32[]{:S(2)}, u32[]{:S(2)}) %all-to-all-start.1) | async-done | bytes 12582944 | tf_op jit(solution)/shard_map/all_to_all | solution.py:30
  393.4 2.2 constant_dynamic-slice_fusion
  395.6 1.6 bitcast_select_fusion
  397.2 0.6 copy-done.1
  397.8 1.5 pad_maximum_fusion
  399.3 1.3 copy-done.4
  400.7 1.6 fusion.62
  402.3 1.0 fusion.9
  403.3 2.0 copy-done.2
  405.3 0.6 exponential_add_fusion
  406.0 3.4 fusion.63
  409.4 1.0 fusion.8
  410.5 1.9 copy-done.3
  412.4 0.6 exponential_add_fusion.1
  413.2 6.3 %fusion.58 = (f32[256]{0:T(256)S(1)}, f32[256,7168]{0,1:T(8,128)}) fusion(pred[256,7168]{0,1:T(32,128)(4,1)} %copy.49, bf16[256,128]{1,0:T(8,128)(2,1)S(1)} %reshape_squeeze.15, bf16[4096,512]{1,0:T(8,128)(2,1)} %param.10, bf16[3072,512]{1,0:T(8,128)(2,1)S(1)} %bitcast_select_fusion), kind=kOutput, calls=%fused_computation.115 | convolution fusion | flops 478936832 | bytes 16581632 | tf_op jit(solution)/shard_map/dot_general | solution.py:63
  419.8 4.1 fusion.11
  424.0 5.1 %fusion.15 = f32[256,128]{1,0:T(8,128)S(1)} fusion(bf16[7168,128]{1,0:T(8,128)(2,1)} %pad_maximum_fusion, f32[256,7168]{0,1:T(8,128)} %get-tuple-element.21, f32[256]{0:T(256)S(1)} %add.104, f32[256]{0:T(256)S(1)} %max.66), kind=kOutput, calls=%fused_computation.36 | convolution fusion | flops 475267072 | bytes 9308160 | tf_op jit(solution)/shard_map/dot_general | solution.py:84
  429.2 0.2 fusion.25
  429.5 6.3 %fusion.60 = (f32[256]{0:T(256)S(1)}, f32[256,7168]{0,1:T(8,128)}) fusion(pred[256,7168]{0,1:T(32,128)(4,1)} %copy.49, bf16[256,128]{1,0:T(8,128)(2,1)S(1)} %reshape_squeeze.14, bf16[4096,512]{1,0:T(8,128)(2,1)} %param.10, bf16[3072,512]{1,0:T(8,128)(2,1)S(1)} %bitcast_select_fusion), kind=kOutput, calls=%fused_computation.117 | convolution fusion | flops 478936832 | bytes 16581632 | tf_op jit(solution)/shard_map/dot_general | solution.py:63
  436.1 4.3 fusion.10
  440.6 4.8 %fusion.14 = f32[256,128]{1,0:T(8,128)S(1)} fusion(f32[256,7168]{0,1:T(8,128)} %get-tuple-element.25, f32[256]{0:T(256)S(1)} %add.101, f32[256]{0:T(256)S(1)} %max.64, bf16[4096,512]{1,0:T(8,128)(2,1)} %param.10, bf16[3072,512]{1,0:T(8,128)(2,1)S(1)} %bitcast_select_fusion), kind=kOutput, calls=%fused_computation.35 | convolution fusion | flops 478937088 | bytes 14813184 | tf_op jit(solution)/shard_map/dot_general | solution.py:84
  445.4 0.2 fusion.26
  445.8 5.1 %fusion.24 = bf16[256,128]{1,0:T(8,128)(2,1)S(1)} fusion(bf16[7168,128]{1,0:T(8,128)(2,1)} %pad_maximum_fusion, f32[256,7168]{0,1:T(8,128)} %copy-done.2, f32[256]{0:T(256)} %exponential_add_fusion, f32[256]{0:T(256)} %copy-done.12, f32[32,128]{1,0:T(8,128)S(1)} %copy-done.9, f32[32,8]{1,0:T(8,128)S(1)} %fusion.46), kind=kOutput, calls=%fused_computation.49 | convolution fusion | flops 475365376 | bytes 9260032 | tf_op jit(solution)/shard_map/dot_general | solution.py:84
  450.9 4.8 %fusion.23 = bf16[256,128]{1,0:T(8,128)(2,1)S(1)} fusion(f32[256,7168]{0,1:T(8,128)} %copy-done.3, f32[256]{0:T(256)S(1)} %copy-done.17, f32[256]{0:T(256)S(1)} %copy-done.14, f32[32,128]{1,0:T(8,128)S(1)} %get-tuple-element.12, f32[32,8]{1,0:T(8,128)S(1)} %fusion.47, bf16[4096,512]{1,0:T(8,128)(2,1)} %param.10, bf16[3072,512]{1,0:T(8,128)(2,1)S(1)} %bitcast_select_fusion), kind=kOutput, calls=%fused_computation.48 | convolution fusion | flops 479035392 | bytes 14765056 | tf_op jit(solution)/shard_map/dot_general | solution.py:84
  455.8 0.7 maximum_maximum_fusion
  (90 shorter events, 2.4 us)
Async XLA Ops:
  25.9 5.0 %copy-start.18 = (s32[64]{0:T(128)S(1)}, s32[64]{0:T(128)}, u32[]{:S(2)}) copy-start(s32[64]{0:T(128)} %param.9) | copy-start | bytes 772
  25.9 40.5 %all-to-all-start = ((bf16[4,2,196608]{2,1,0:T(2,128)(2,1)}), bf16[4,2,196608]{2,1,0:T(2,128)(2,1)S(1)}, u32[]{:S(2)}, u32[]{:S(2)}) async-start(bf16[4,2,196608]{2,1,0:T(2,128)(2,1)} %reshape.386), calls=%async_computation | async-start | bytes 6291456 | tf_op jit(solution)/shard_map/all_to_all | solution.py:16
  107.1 15.0 %copy-start.19 = (s32[64]{0:T(128)S(1)}, s32[64]{0:T(128)}, u32[]{:S(2)}) copy-start(s32[64]{0:T(128)} %param.8) | copy-start | bytes 772
  107.1 18.2 %copy-start.20 = (s32[1,31]{1,0:T(1,128)S(1)}, s32[1,31]{1,0:T(1,128)}, u32[]{:S(2)}) copy-start(s32[1,31]{1,0:T(1,128)} %param.11) | copy-start | bytes 376
  107.1 286.3 %all-to-all-start.1 = ((bf16[64,192,512]{2,1,0:T(8,128)(2,1)}), bf16[64,192,512]{2,1,0:T(8,128)(2,1)}, u32[]{:S(2)}, u32[]{:S(2)}) async-start(bf16[64,192,512]{2,1,0:T(8,128)(2,1)} %broadcast_select_fusion), calls=%async_computation.1 | async-start | bytes 25165824 | tf_op jit(solution)/shard_map/all_to_all | solution.py:30
  122.1 8.6 %copy-start.5 = (bf16[2,32,2048]{2,1,0:T(8,128)(2,1)S(1)}, bf16[2,32,2048]{2,1,0:T(8,128)(2,1)}, u32[]{:S(2)}) copy-start(bf16[2,32,2048]{2,1,0:T(8,128)(2,1)} %param.12) | copy-start | bytes 786436
  125.5 5.3 %copy-start.6 = (bf16[2,32,512]{2,1,0:T(8,128)(2,1)S(1)}, bf16[2,32,512]{2,1,0:T(8,128)(2,1)}, u32[]{:S(2)}) copy-start(bf16[2,32,512]{2,1,0:T(8,128)(2,1)} %param.13) | copy-start | bytes 196612
  395.6 2.2 copy-start.1
  397.8 53.1 %copy-start = (bf16[3072,512]{1,0:T(8,128)(2,1)}, bf16[3072,512]{1,0:T(8,128)(2,1)S(1)}, u32[]{:S(2)}) copy-start(bf16[3072,512]{1,0:T(8,128)(2,1)S(1)} %bitcast_select_fusion) | copy-start | bytes 9437188
  397.8 2.8 copy-start.4
  402.2 3.0 copy-start.2
  402.3 3.0 copy-start.12
  409.4 3.0 copy-start.3
  409.4 3.0 copy-start.13
  413.1 6.4 %copy-start.16 = (f32[256]{0:T(256)S(1)}, f32[256]{0:T(256)}, u32[]{:S(2)}) copy-start(f32[256]{0:T(256)} %reduce_max.84) | copy-start | bytes 3076
  413.2 6.5 %copy-start.8 = (f32[32,8,2]{1,2,0:T(2,128)S(1)}, f32[32,8,2]{1,2,0:T(2,128)}, u32[]{:S(2)}) copy-start(f32[32,8,2]{1,2,0:T(2,128)} %get-tuple-element.23) | copy-start | bytes 6148
  424.0 5.2 %copy-start.11 = (bf16[2,32,128]{2,1,0:T(8,128)(2,1)S(1)}, bf16[2,32,128]{2,1,0:T(8,128)(2,1)}, u32[]{:S(2)}) copy-start(bf16[2,32,128]{2,1,0:T(8,128)(2,1)} %get-tuple-element.19) | copy-start | bytes 49156
  429.5 6.4 %copy-start.15 = (f32[256]{0:T(256)S(1)}, f32[256]{0:T(256)}, u32[]{:S(2)}) copy-start(f32[256]{0:T(256)} %reduce_max.80) | copy-start | bytes 3076
  429.5 6.5 %copy-start.7 = (f32[32,8,2]{1,2,0:T(2,128)S(1)}, f32[32,8,2]{1,2,0:T(2,128)}, u32[]{:S(2)}) copy-start(f32[32,8,2]{1,2,0:T(2,128)} %get-tuple-element.27) | copy-start | bytes 6148
  440.5 4.9 %copy-start.10 = (bf16[2,32,128]{2,1,0:T(8,128)(2,1)S(1)}, bf16[2,32,128]{2,1,0:T(8,128)(2,1)}, u32[]{:S(2)}) copy-start(bf16[2,32,128]{2,1,0:T(8,128)(2,1)} %get-tuple-element.16) | copy-start | bytes 49156
  440.5 5.2 %copy-start.9 = (f32[32,128]{1,0:T(8,128)S(1)}, f32[32,128]{1,0:T(8,128)}, u32[]{:S(2)}) copy-start(f32[32,128]{1,0:T(8,128)} %get-tuple-element.15) | copy-start | bytes 49156
  445.7 5.2 %copy-start.14 = (f32[256]{0:T(256)S(1)}, f32[256]{0:T(256)}, u32[]{:S(2)}) copy-start(f32[256]{0:T(256)} %copy-done.13) | copy-start | bytes 3076
  445.7 5.2 %copy-start.17 = (f32[256]{0:T(256)S(1)}, f32[256]{0:T(256)}, u32[]{:S(2)}) copy-start(f32[256]{0:T(256)} %exponential_add_fusion.1) | copy-start | bytes 3076
where the time goes:
time: 463 us; the launch traced here: 457 us
  waiting for transfers between devices  293 us (63%)
  local copies, waits for them, and re-layouts  70.7 us (15%)
  matrix products  39.9 us (9%)
  other arithmetic  29.7 us (6%)
  starting transfers between devices  19.9 us (4%)
    all_to_all x1, waiting for transfers between devices, per_device(): lax.all_to_all(outgoing, ('seq', 'rep'), split_axis=0, concat_axis=1, til...  257 us
    unnamed x50, local copies, waits for them, and re-layouts  41.1 us
    all_to_all x1, waiting for transfers between devices, per_device(): lax.all_to_all(prompt_kv, 'kvh', split_axis=2, concat_axis=1, tiled=True)  35.3 us
    dot_general x4, matrix products, per_device(): mixed = jnp.dot(rounded_cache, values, preferred_element_type=jnp.float32)  19.9 us
    dot_general x4, matrix products, per_device(): lax.dot_general(query, head_keys, (((1,), (1,)), ((), ())), preferred_ele...  17.7 us
    all_to_all x1, starting transfers between devices, per_device(): lax.all_to_all(outgoing, ('seq', 'rep'), split_axis=0, concat_axis=1, til...  14.9 us
    all_to_all x2, local copies, waits for them, and re-layouts, per_device(): lax.all_to_all(prompt_kv, 'kvh', split_axis=2, concat_axis=1, tiled=True)  12.9 us
    select_n x2, other arithmetic, per_device(): outgoing = jnp.take(pieces, source, axis=0)  10.9 us
  transfers between devices with their start and end apart: 2, of which 2 were waited for; matrix products, arithmetic and copies ran while one was open for 3% of the time, Pallas kernels for 0%

commit v1 on v0

v1 whole, which is shorter than its diff:
```python
import functools
import jax
import jax.numpy as jnp
from jax import lax
from jax.experimental import pallas as pl
from jax.experimental.pallas import tpu as pltpu
from jax.sharding import PartitionSpec as P

HD = 128
STEPS = 2
CORES = 2
BLK = 16
NEG = -1e30
MESH = pl.DeviceIdType.MESH
EXP2_SCALE = (HD ** -0.5) * 1.4426950408889634
BF16 = jnp.bfloat16
F32 = jnp.float32
NT = (((1,), (1,)), ((), ()))


def wrap(value, size):
    return lax.rem(value + size, size)


def iota(shape, dim):
    return lax.broadcasted_iota(jnp.int32, shape, dim)


def kernel(cfg, prompt, plen_s, rgroup_s, plen_v, rgroup_v, res, rlen, queries, fresh, att_out, land_out, *scratch):
    n_seq, n_kvh, n_rep = cfg["mesh"]
    n_z = n_seq // CORES
    n_req, shard, _ = prompt.shape
    width = land_out.shape[3]
    blocks = shard // BLK
    per_rep = n_req // n_rep
    heads = width // (2 * HD)
    rows = queries.shape[1]
    gqa = queries.shape[2] // (heads * HD)
    q_rows = STEPS * gqa * rows
    res_tok = res.shape[0]
    chunks = cfg["chunks"]
    nc = len(chunks)
    it = iter(scratch)
    pv = [next(it) for _ in range(blocks)]
    s1 = [next(it) for _ in chunks]
    r1 = [next(it) for _ in chunks]
    s2 = [next(it) for _ in chunks]
    land, kcat, vcat, qcat, qv, fv, accs, sums, maxs, attv, tab_v, tab_s = (next(it) for _ in range(12))
    load_sem, send1, recv1, send2, recv2, out_sem = (next(it) for _ in range(6))

    seq, kvh, rep = lax.axis_index("seq"), lax.axis_index("kvh"), lax.axis_index("rep")
    zed, core = seq // CORES, lax.rem(seq, CORES)
    plane = [(a, b) for a in (2, 1, 3, 0) for b in (2, 1, 3, 0) if (a, b) != (0, 0)]
    line = [(a, b) for a in (4, 3, 5, 2, 6, 1, 7, 0) for b in (0, 1) if (a, b) != (0, 0)]

    def plane_peer(off):
        return lax.rem(kvh + off[0], n_kvh), lax.rem(rep + off[1], n_rep)

    def line_peer(off):
        return lax.rem(zed + off[0], n_z) * CORES + lax.rem(core + off[1], CORES)

    loads = [pltpu.make_async_copy(prompt.at[:, pl.ds(b * BLK, BLK), :], pv[b], load_sem.at[b]) for b in range(blocks)]
    for copy in loads:
        copy.start()
    others = []
    for h in range(heads):
        for at, dst in ((0, kcat), (HD, vcat)):
            others.append((res.at[:, pl.ds(2 * h * HD + at, HD)], dst.at[h, pl.ds(0, res_tok), pl.ds(0, HD)]))
    others += [(queries, qv), (fresh, fv)]
    others = [pltpu.make_async_copy(a, b, load_sem.at[blocks + i]) for i, (a, b) in enumerate(others)]
    for copy in others:
        copy.start()

    barrier = pltpu.get_barrier_semaphore()
    for off in plane:
        k2, r2 = plane_peer(off)
        pl.semaphore_signal(barrier, inc=1, device_id=(seq, k2, r2), device_id_type=MESH)
    for off in line:
        pl.semaphore_signal(barrier, inc=1, device_id=(line_peer(off), kvh, rep), device_id_type=MESH)

    packed, power = [0] * n_rep, [1] * n_rep
    for q in range(n_req):
        to_rep = lax.rem(rgroup_s[rep * n_req + q], n_rep)
        for d in range(n_rep):
            hit = to_rep == lax.rem(rep + d, n_rep)
            packed[d] = packed[d] + jnp.where(hit, power[d] * q, 0)
            power[d] = jnp.where(hit, power[d] * n_req, power[d])
    bits = n_req.bit_length() - 1

    def request_at(d, j):
        return (packed[d] >> (bits * j)) & (n_req - 1)

    def send_plane(c):
        b, c0, w = chunks[c]
        for i, off in enumerate(plane + [(0, 0)]):
            k2, r2 = plane_peer(off)
            cols = pl.ds(pl.multiple_of(k2 * width + c0, HD), w)
            for j in range(per_rep):
                piece = pv[b][request_at(off[1], j), :, cols]
                if off == (0, 0):
                    r1[c][(kvh * n_rep + rep) * per_rep + j] = piece
                else:
                    s1[c][i * per_rep + j] = piece
        if c == 0:
            pl.semaphore_wait(barrier, len(plane) + len(line))
        for i, off in enumerate(plane):
            k2, r2 = plane_peer(off)
            pltpu.make_async_remote_copy(
                src_ref=s1[c].at[pl.ds(i * per_rep, per_rep)],
                dst_ref=r1[c].at[pl.ds((kvh * n_rep + rep) * per_rep, per_rep)],
                send_sem=send1.at[c],
                recv_sem=recv1.at[c],
                device_id=(seq, k2, r2),
                device_id_type=MESH,
            ).start()

    landed_at = lambda c, s, n: land.at[pl.ds(s, n), :, pl.ds(chunks[c][0] * BLK, BLK), pl.ds(chunks[c][1], chunks[c][2])]

    def send_line(c):
        b, c0, w = chunks[c]
        for i, off in enumerate(line + [(0, 0)]):
            s_to = line_peer(off)
            slot, length = jnp.clip(tab_s[s_to, 0], 0, n_rep * per_rep - 1), tab_s[s_to, 1]
            for k in range(n_kvh):
                piece = r1[c][k * n_rep * per_rep + slot]
                at = (seq * n_kvh + k) * shard + b * BLK + iota((BLK, w), 0)
                piece = jnp.where(at < length, piece, jnp.zeros_like(piece))
                if off == (0, 0):
                    land[seq, k, pl.ds(b * BLK, BLK), pl.ds(c0, w)] = piece
                else:
                    s2[c][i, k] = piece
        for i, off in enumerate(line):
            pltpu.make_async_remote_copy(
                src_ref=s2[c].at[pl.ds(i, 1)],
                dst_ref=landed_at(c, seq, 1),
                send_sem=send2.at[c],
                recv_sem=recv2.at[c],
                device_id=(line_peer(off), kvh, rep),
                device_id_type=MESH,
            ).start()

    for c in range(nc):
        if c == 0 or chunks[c][0] != chunks[c - 1][0]:
            loads[chunks[c][0]].wait()
        send_plane(c)

    total_req = rgroup_v.shape[1]
    groups = rgroup_v[...]
    mine = (lax.rem(groups, n_rep) == rep).astype(BF16)
    earlier = (iota((total_req, total_req), 0) < iota((total_req, total_req), 1)).astype(BF16)
    slots = jnp.dot(jnp.broadcast_to(mine, (n_seq, total_req)), earlier, preferred_element_type=F32)
    goes = jnp.broadcast_to(groups, (n_seq, total_req)) == iota((n_seq, total_req), 0) * n_rep + rep
    slot_of = jnp.sum(jnp.where(goes, slots, 0.0), axis=1, keepdims=True)
    len_of = jnp.sum(jnp.where(goes, plen_v[...].astype(F32), 0.0), axis=1, keepdims=True)
    lane = iota((n_seq, HD), 1)
    tab_v[...] = jnp.where(lane == 0, slot_of, len_of).astype(jnp.int32)
    to_smem = pltpu.make_async_copy(tab_v, tab_s, load_sem.at[blocks + len(others)])
    to_smem.start()
    to_smem.wait()

    for c in range(nc):
        pltpu.make_async_copy(
            r1[c].at[pl.ds(0, len(plane) * per_rep)], r1[c].at[pl.ds(0, len(plane) * per_rep)], recv1.at[c]
        ).wait()
        send_line(c)

    for copy in others:
        copy.wait()
    n_keys = kcat.shape[1]
    lens = rlen[...].astype(F32)
    diagonal = jnp.where(iota((rows, rows - 1), 0) == iota((rows, rows - 1), 1), lens, 0.0)
    column = jnp.sum(diagonal, axis=1, keepdims=True)
    above = iota((rows, HD), 0) - iota((rows, HD), 1)
    ends = jnp.sum(jnp.where(above <= 0, column, 0.0), axis=0, keepdims=True).astype(jnp.int32)
    starts = jnp.sum(jnp.where(above < 0, column, 0.0), axis=0, keepdims=True).astype(jnp.int32)

    def hide(i, carry):
        key = i * 256 + iota((256, HD), 0)
        hidden = ((key < starts) | (key >= ends)) & (iota((256, HD), 1) < rows)
        hidden = hidden.astype(F32).astype(BF16)
        at = pl.ds(pl.multiple_of(i * 256, 256), 256)
        for h in range(heads):
            kcat[h, at, pl.ds(HD, HD)] = hidden
            vcat[h, at, pl.ds(HD, HD)] = jnp.ones((256, HD), BF16)
        return carry

    lax.fori_loop(0, res_tok // 256, hide, 0)
    rest = n_keys - res_tok
    key, lane = iota((rest, HD), 0), iota((rest, HD), 1)
    hidden = ((lane < rows) & (lane != lax.rem(key, rows))) | ((lane == rows) & (key >= rows)) | (
        (lane == rows + 1) & (key >= STEPS * rows)
    )
    hidden = hidden.astype(F32).astype(BF16)
    pad = jnp.zeros((rest - STEPS * rows, HD), BF16)
    for h in range(heads):
        kcat[h, pl.ds(res_tok, rest), pl.ds(HD, HD)] = hidden
        vcat[h, pl.ds(res_tok, rest), pl.ds(HD, HD)] = jnp.ones((rest, HD), BF16)
        for at, dst in ((0, kcat), (HD, vcat)):
            for u in range(STEPS):
                dst[h, pl.ds(res_tok + u * rows, rows), pl.ds(0, HD)] = fv[u, :, pl.ds(2 * h * HD + at, HD)]
            dst[h, pl.ds(res_tok + STEPS * rows, rest - STEPS * rows), pl.ds(0, HD)] = pad
    row, lane = iota((rows, HD), 0), iota((rows, HD), 1)
    for t in range(STEPS):
        aside = (lane == row) | (lane == rows + 1)
        if t == 0:
            aside = aside | (lane == rows)
        aside = jnp.where(aside, NEG, 0.0).astype(BF16)
        for h in range(heads):
            for g in range(gqa):
                at = pl.ds((t * gqa + g) * rows, rows)
                qcat[h, at, pl.ds(0, HD)] = qv[t, :, pl.ds((h * gqa + g) * HD, HD)]
                qcat[h, at, pl.ds(HD, HD)] = aside

    q_tile = cfg["q_tile"]
    tiles = q_rows // q_tile

    def attend(i, carry):
        h, at = i // tiles, pl.ds(pl.multiple_of(lax.rem(i, tiles) * q_tile, q_tile), q_tile)
        scores = lax.dot_general(qcat[h, at, :], kcat[h], NT, preferred_element_type=F32)
        top = jnp.max(scores, axis=1, keepdims=True)
        weights = jnp.exp2((scores - top) * EXP2_SCALE).astype(BF16)
        mixed = jnp.dot(weights, vcat[h], preferred_element_type=F32)
        accs[h, at, :] = mixed[:, :HD]
        sums[h, at, :] = mixed[:, HD:]
        maxs[h, at, :] = jnp.broadcast_to(top, (q_tile, HD))
        return carry

    lax.fori_loop(0, heads * tiles, attend, 0)

    few = STEPS * gqa
    pick = (iota((few, q_rows), 1) == iota((few, q_rows), 0) * rows + (rows - 1)).astype(F32).astype(BF16)
    last = pl.ds(rows - 1, few, stride=rows)
    own_len = tab_s[seq, 1]
    asks, parts = [], []
    for h in range(heads):
        asks.append(jnp.dot(pick, qcat[h, :, pl.ds(0, HD)], preferred_element_type=F32).astype(BF16))
        parts.append([(maxs[h, last, :], sums[h, last, :], accs[h, last, :])])
    for h in range(heads):
        accs[h] = accs[h] / sums[h]

    keys_blk = n_seq * n_kvh * BLK
    n_at = iota((few, keys_blk), 1)
    n_at = (n_at // BLK) * shard + lax.rem(n_at, BLK)
    outs = []
    arrived = set()
    for c, (b, c0, w) in enumerate(chunks):
        pltpu.make_async_copy(landed_at(c, 0, len(line)), landed_at(c, 0, len(line)), recv2.at[c]).wait()
        out = pltpu.make_async_copy(
            landed_at(c, 0, n_seq),
            land_out.at[:, :, pl.ds(b * BLK, BLK), pl.ds(c0, w)],
            out_sem.at[c],
        )
        out.start()
        outs.append(out)
        arrived |= {(b, at) for at in range(c0, c0 + w, HD)}
        for h in range(heads):
            k_at, v_at = 2 * h * HD, (2 * h + 1) * HD
            if not {(b, k_at), (b, v_at)} <= arrived:
                continue
            arrived -= {(b, k_at), (b, v_at)}
            keys = land[:, :, pl.ds(b * BLK, BLK), pl.ds(k_at, HD)].reshape(keys_blk, HD)
            values = land[:, :, pl.ds(b * BLK, BLK), pl.ds(v_at, HD)].reshape(keys_blk, HD)
            scores = lax.dot_general(asks[h], keys, NT, preferred_element_type=F32)
            scores = jnp.where(n_at + b * BLK < own_len, scores, NEG)
            top = jnp.max(scores, axis=1, keepdims=True)
            weights = jnp.exp2((scores - top) * EXP2_SCALE)
            total = jnp.sum(weights, axis=1, keepdims=True)
            mixed = jnp.dot(weights.astype(BF16), values, preferred_element_type=F32)
            parts[h].append((top, total, mixed))
    for h in range(heads):
        top = functools.reduce(jnp.maximum, [m for m, _, _ in parts[h]])
        total, mixed = 0.0, 0.0
        for m, l, a in parts[h]:
            factor = jnp.exp2((m - top) * EXP2_SCALE)
            total, mixed = total + factor * l, mixed + factor * a
        accs[h, last, :] = mixed / total
        for t in range(STEPS):
            for g in range(gqa):
                attv[t, :, pl.ds((h * gqa + g) * HD, HD)] = accs[h, pl.ds((t * gqa + g) * rows, rows), :].astype(BF16)
    out = pltpu.make_async_copy(attv, att_out, out_sem.at[nc])
    out.start()
    outs.append(out)
    for c in range(nc):
        pltpu.make_async_copy(s1[c], s1[c], send1.at[c]).wait()
        pltpu.make_async_copy(s2[c], s2[c], send2.at[c]).wait()
    for out in outs:
        out.wait()


def per_device(mesh_shape, prompt_kv, prompt_len, request_group, res_kv, res_len, queries, step_kv):
    n_seq, n_kvh, n_rep = mesh_shape
    n_req, shard, all_cols = prompt_kv.shape
    width = all_cols // n_kvh
    per_rep = n_req // n_rep
    heads = width // (2 * HD)
    blocks = shard // BLK
    rows, q_cols = queries.shape[1:]
    q_rows = STEPS * rows * (q_cols // (heads * HD))
    chunks = [(b, c0, 2 * HD) for b in range(blocks) for c0 in range(0, width, 2 * HD)]
    n_keys = res_kv.shape[0] + 256
    cfg = dict(mesh=mesh_shape, chunks=chunks, q_tile=128)
    near, far = n_kvh * n_rep, n_seq
    v = lambda shape, dtype=BF16: pltpu.VMEM(shape, dtype)
    dma = lambda n: pltpu.SemaphoreType.DMA((n,))
    scratch = (
        [v((n_req, BLK, all_cols)) for _ in range(blocks)]
        + [v(((near - 1) * per_rep, BLK, w)) for _, _, w in chunks]
        + [v((near * per_rep, BLK, w)) for _, _, w in chunks]
        + [v((far - 1, n_kvh, BLK, w)) for _, _, w in chunks]
        + [
            v((n_seq, n_kvh, shard, width)),
            v((heads, n_keys, 2 * HD)),
            v((heads, n_keys, 2 * HD)),
            v((heads, q_rows, 2 * HD)),
            v(queries.shape),
            v(step_kv.shape),
            v((heads, q_rows, HD), F32),
            v((heads, q_rows, HD), F32),
            v((heads, q_rows, HD), F32),
            v(queries.shape),
            v((n_seq, HD), jnp.int32),
            pltpu.SMEM((n_seq, HD), jnp.int32),
        ]
        + [dma(blocks + 2 * heads + 3)]
        + [dma(len(chunks))] * 4
        + [dma(len(chunks) + 1)]
    )
    spec = lambda space: pl.BlockSpec(memory_space=space)
    attention, landed = pl.pallas_call(
        functools.partial(kernel, cfg),
        out_shape=(
            jax.ShapeDtypeStruct(queries.shape, BF16),
            jax.ShapeDtypeStruct((n_seq, n_kvh, shard, width), BF16),
        ),
        in_specs=[spec(s) for s in (pl.ANY, pltpu.SMEM, pltpu.SMEM, pltpu.VMEM, pltpu.VMEM, pl.ANY, pltpu.VMEM, pl.ANY, pl.ANY)],
        out_specs=(spec(pl.ANY), spec(pl.ANY)),
        scratch_shapes=scratch,
        compiler_params=pltpu.CompilerParams(collective_id=0, has_side_effects=True, vmem_limit_bytes=56 << 20),
    )(
        prompt_kv,
        prompt_len,
        request_group,
        prompt_len.reshape(1, -1),
        request_group.reshape(1, -1),
        res_kv,
        res_len,
        queries,
        step_kv,
    )
    return attention, landed.reshape(n_seq * n_kvh * shard, width)


def solution(mesh):
    in_specs = (
        P("rep", ("seq", "kvh"), None),
        P(),
        P(),
        P(("seq", "rep"), "kvh"),
        P(("seq", "rep"), None),
        P(None, ("seq", "rep"), "kvh"),
        P(None, ("seq", "rep"), "kvh"),
    )
    out_specs = (P(None, ("seq", "rep"), "kvh"), P(("seq", "rep"), "kvh"))
    shape = tuple(mesh.shape[a] for a in ("seq", "kvh", "rep"))
    return jax.shard_map(
        functools.partial(per_device, shape), mesh=mesh, in_specs=in_specs, out_specs=out_specs, check_vma=False
    )
```

time: 463 us -> 97.1 us (0.21); the launches traced: 457 us -> 97 us
  waiting for transfers between devices: 293 us -> 0 us
  Pallas kernels: 0 us -> 90.9 us
  local copies, waits for them, and re-layouts: 70.7 us -> 5.42 us
  matrix products: 39.9 us -> 0 us
  other arithmetic: 29.7 us -> 0 us
  starting transfers between devices: 19.9 us -> 0 us
    all_to_all x2 -> x0, waiting for transfers between devices: 293 us -> none  [the longest x1 257 us: per_device(): lax.all_to_all(outgoing, ('seq', 'rep'), split_axis=0, concat_axis=1, til...]
    pallas_call x0 -> x1, Pallas kernels: none -> 90.9 us  [per_device(): pl.pallas_call(functools.partial(kernel, cfg), out_shape=(jax.ShapeDtypeS...]
    dot_general x14 -> x0, matrix products: 39.9 us -> none  [the longest x4 19.9 us: per_device(): mixed = jnp.dot(rounded_cache, values, preferred_element_type=jnp.float32)]
    unnamed x50 -> x2, local copies, waits for them, and re-layouts: 41.1 us -> 5.42 us
    all_to_all x2 -> x0, starting transfers between devices: 19.9 us -> none  [the longest x1 14.9 us: per_device(): lax.all_to_all(outgoing, ('seq', 'rep'), split_axis=0, concat_axis=1, til...]
    all_to_all x2 -> x0, local copies, waits for them, and re-layouts: 12.9 us -> none  [per_device(): lax.all_to_all(prompt_kv, 'kvh', split_axis=2, concat_axis=1, tiled=True)]
    select_n x3 -> x0, other arithmetic: 12.5 us -> none  [the longest x2 10.9 us: per_device(): outgoing = jnp.take(pieces, source, axis=0)]
    reduce_sum x8 -> x0, other arithmetic: 11.4 us -> none  [the longest x6 10.7 us: per_device(): row_total = jnp.sum(weight_cache, axis=1) + jnp.sum(weight_fresh, axis=1)]
  transfers between devices with their start and end apart: 2 -> 0, of which waited for: 2 -> 0; matrix products, arithmetic and copies ran while one was open for 3% -> 0% of each run, Pallas kernels for 0% -> 0%
where the time goes in v1:
time: 97.1 us; the launch traced here: 97 us
  Pallas kernels  90.9 us (94%)
  local copies, waits for them, and re-layouts  5.42 us (6%)
    pallas_call x1, Pallas kernels, per_device(): pl.pallas_call(functools.partial(kernel, cfg), out_shape=(jax.ShapeDtypeS...  90.9 us
    unnamed x2, local copies, waits for them, and re-layouts  5.42 us

profile of v1, /device:TPU:1, one launch (start us, length us, event | category | flops | bytes accessed | tf_op | source)
XLA Modules:
  0.0 97.0 jit_solution(3329658613603751151)
XLA Ops:
  0.6 90.9 %shard_map.86 = (bf16[2,32,2048]{2,1,0:T(8,128)(2,1)}, bf16[16,4,48,512]{3,2,1,0:T(8,128)(2,1)}) custom-call(bf16[16,48,2048]{2,1,0:T(8,128)(2,1)} %prompt.1, s32[64]{0:T(128)} %plen_s.1, s32[64]{0:T(128)} %rgroup_s.1, s32[1,64]{1,0:T(1,128)} %bitcast.4, s32[1,64]{1,0:T(1,128)} %bitcast.5, bf16[4096,512]{1,0:T(8,128)(2,1)} %res.1, s32[1,31]{1,0:T(1,128)} %rlen.1, ...), custom_call_target="tpu_custom_call" | custom-call | tf_op jit(solution)/shard_map/pallas_call | solution.py:329
  91.5 1.7 %copy.11 = bf16[2,32,2048]{2,1,0:T(8,128)(2,1)} copy(bf16[2,32,2048]{2,1,0:T(8,128)(2,1)} %get-tuple-element.8) | data formatting | bytes 524288
  93.2 3.8 %copy.12 = bf16[3072,512]{1,0:T(8,128)(2,1)} copy(bf16[3072,512]{1,0:T(8,128)(2,1)} %bitcast.3) | data formatting | bytes 6291456

commit v2 on v1

--- a/solution.py
+++ b/solution.py
@@ -16,6 +16,17 @@
 BF16 = jnp.bfloat16
 F32 = jnp.float32
 NT = (((1,), (1,)), ((), ()))
+AHEAD = 4
+ALL = (0, 1, 2, 3)
+CHUNKS = [
+    (0, 0, 128, (0,)),
+    (0, 0, 128, (1,)),
+    (0, 0, 128, (2, 3)),
+    (0, 128, 128, ALL),
+    (0, 256, 256, ALL),
+    (1, 0, 512, ALL),
+    (2, 0, 512, ALL),
+]
 
 
 def wrap(value, size):
@@ -26,11 +37,11 @@
     return lax.broadcasted_iota(jnp.int32, shape, dim)
 
 
-def kernel(cfg, prompt, plen_s, rgroup_s, plen_v, rgroup_v, res, rlen, queries, fresh, att_out, land_out, *scratch):
+def kernel(cfg, prompt, plen_s, rgroup_s, plen_v, rgroup_v, res, rlen, queries, fresh, attv, land, *scratch):
     n_seq, n_kvh, n_rep = cfg["mesh"]
     n_z = n_seq // CORES
     n_req, shard, _ = prompt.shape
-    width = land_out.shape[3]
+    width = land.shape[3]
     blocks = shard // BLK
     per_rep = n_req // n_rep
     heads = width // (2 * HD)
@@ -41,35 +52,52 @@
     chunks = cfg["chunks"]
     nc = len(chunks)
     it = iter(scratch)
-    pv = [next(it) for _ in range(blocks)]
+    pieces = sorted({chunk[:3] for chunk in chunks})
+    pv = [next(it) for _ in pieces]
     s1 = [next(it) for _ in chunks]
     r1 = [next(it) for _ in chunks]
     s2 = [next(it) for _ in chunks]
-    land, kcat, vcat, qcat, qv, fv, accs, sums, maxs, attv, tab_v, tab_s = (next(it) for _ in range(12))
-    load_sem, send1, recv1, send2, recv2, out_sem = (next(it) for _ in range(6))
+    kcat, vcat, qcat, qv, fv, accs, sums, maxs, tab_v, tab_s = (next(it) for _ in range(10))
+    load_sem, send1, recv1, send2, recv2 = (next(it) for _ in range(5))
 
     seq, kvh, rep = lax.axis_index("seq"), lax.axis_index("kvh"), lax.axis_index("rep")
     zed, core = seq // CORES, lax.rem(seq, CORES)
-    plane = [(a, b) for a in (2, 1, 3, 0) for b in (2, 1, 3, 0) if (a, b) != (0, 0)]
+    plane = [(a, b) for a in (2, 3, 1, 0) for b in (2, 1, 3, 0) if (a, b) != (0, 0)]
     line = [(a, b) for a in (4, 3, 5, 2, 6, 1, 7, 0) for b in (0, 1) if (a, b) != (0, 0)]
 
+    kvh_peer = [kvh, kvh + 1 - 2 * lax.rem(kvh, 2), lax.rem(kvh + 2, 4), 3 - kvh]
+
     def plane_peer(off):
-        return lax.rem(kvh + off[0], n_kvh), lax.rem(rep + off[1], n_rep)
+        return kvh_peer[off[0]], lax.rem(rep + off[1], n_rep)
+
+    def first_slab(c):
+        steps = chunks[c][3]
+        return 0 if steps == ALL else 2 - 2 * (kvh // 2) if steps == (2, 3) else kvh_peer[steps[0]]
+
+    def own_place(c):
+        steps = chunks[c][3]
+        return kvh if steps == ALL else lax.rem(kvh, 2) if steps == (2, 3) else 0
 
     def line_peer(off):
         return lax.rem(zed + off[0], n_z) * CORES + lax.rem(core + off[1], CORES)
 
-    loads = [pltpu.make_async_copy(prompt.at[:, pl.ds(b * BLK, BLK), :], pv[b], load_sem.at[b]) for b in range(blocks)]
-    for copy in loads:
+    def loads(p):
+        b, c0, w = pieces[p]
+        return [
+            pltpu.make_async_copy(
+                prompt.at[:, pl.ds(b * BLK, BLK), pl.ds(k * width + c0, w)], pv[p].at[k], load_sem.at[p * n_kvh + k]
+            )
+            for k in range(n_kvh)
+        ]
+
+    for copy in loads(0):
         copy.start()
     others = []
     for h in range(heads):
         for at, dst in ((0, kcat), (HD, vcat)):
             others.append((res.at[:, pl.ds(2 * h * HD + at, HD)], dst.at[h, pl.ds(0, res_tok), pl.ds(0, HD)]))
     others += [(queries, qv), (fresh, fv)]
-    others = [pltpu.make_async_copy(a, b, load_sem.at[blocks + i]) for i, (a, b) in enumerate(others)]
-    for copy in others:
-        copy.start()
+    others = [pltpu.make_async_copy(a, b, load_sem.at[len(pieces) * n_kvh + i]) for i, (a, b) in enumerate(others)]
 
     barrier = pltpu.get_barrier_semaphore()
     for off in plane:
@@ -91,58 +119,66 @@
         return (packed[d] >> (bits * j)) & (n_req - 1)
 
     def send_plane(c):
-        b, c0, w = chunks[c]
-        for i, off in enumerate(plane + [(0, 0)]):
+        source, offs = pv[pieces.index(chunks[c][:3])], [off for off in plane if off[0] in chunks[c][3]]
+        place = pl.ds((own_place(c) * n_rep + rep) * per_rep, per_rep)
+        for i, off in enumerate(offs):
             k2, r2 = plane_peer(off)
-            cols = pl.ds(pl.multiple_of(k2 * width + c0, HD), w)
             for j in range(per_rep):
-                piece = pv[b][request_at(off[1], j), :, cols]
-                if off == (0, 0):
-                    r1[c][(kvh * n_rep + rep) * per_rep + j] = piece
-                else:
-                    s1[c][i * per_rep + j] = piece
+                s1[c][i * per_rep + j] = source[k2, request_at(off[1], j)]
+        if 0 in chunks[c][3]:
+            for j in range(per_rep):
+                r1[c][(own_place(c) * n_rep + rep) * per_rep + j] = source[kvh, request_at(0, j)]
         if c == 0:
             pl.semaphore_wait(barrier, len(plane) + len(line))
-        for i, off in enumerate(plane):
+        for i, off in enumerate(offs):
             k2, r2 = plane_peer(off)
             pltpu.make_async_remote_copy(
                 src_ref=s1[c].at[pl.ds(i * per_rep, per_rep)],
-                dst_ref=r1[c].at[pl.ds((kvh * n_rep + rep) * per_rep, per_rep)],
+                dst_ref=r1[c].at[place],
                 send_sem=send1.at[c],
                 recv_sem=recv1.at[c],
                 device_id=(seq, k2, r2),
                 device_id_type=MESH,
             ).start()
 
-    landed_at = lambda c, s, n: land.at[pl.ds(s, n), :, pl.ds(chunks[c][0] * BLK, BLK), pl.ds(chunks[c][1], chunks[c][2])]
+    def landed_at(c, s, n, k):
+        b, c0, w, steps = chunks[c]
+        return land.at[pl.ds(s, n), pl.ds(k, len(steps)), pl.ds(b * BLK, BLK), pl.ds(c0, w)]
 
     def send_line(c):
-        b, c0, w = chunks[c]
+        b, c0, w, steps = chunks[c]
+        first = first_slab(c)
         for i, off in enumerate(line + [(0, 0)]):
             s_to = line_peer(off)
             slot, length = jnp.clip(tab_s[s_to, 0], 0, n_rep * per_rep - 1), tab_s[s_to, 1]
-            for k in range(n_kvh):
+            for k in range(len(steps)):
                 piece = r1[c][k * n_rep * per_rep + slot]
-                at = (seq * n_kvh + k) * shard + b * BLK + iota((BLK, w), 0)
+                at = (seq * n_kvh + first + k) * shard + b * BLK + iota((BLK, w), 0)
                 piece = jnp.where(at < length, piece, jnp.zeros_like(piece))
                 if off == (0, 0):
-                    land[seq, k, pl.ds(b * BLK, BLK), pl.ds(c0, w)] = piece
+                    land[seq, first + k, pl.ds(b * BLK, BLK), pl.ds(c0, w)] = piece
                 else:
                     s2[c][i, k] = piece
         for i, off in enumerate(line):
             pltpu.make_async_remote_copy(
                 src_ref=s2[c].at[pl.ds(i, 1)],
-                dst_ref=landed_at(c, seq, 1),
+                dst_ref=landed_at(c, seq, 1, first),
                 send_sem=send2.at[c],
                 recv_sem=recv2.at[c],
                 device_id=(line_peer(off), kvh, rep),
                 device_id_type=MESH,
             ).start()
 
-    for c in range(nc):
-        if c == 0 or chunks[c][0] != chunks[c - 1][0]:
-            loads[chunks[c][0]].wait()
-        send_plane(c)
+    loaded = set()
+
+    def feed(c):
+        if c < nc:
+            p = pieces.index(chunks[c][:3])
+            if p not in loaded:
+                loaded.add(p)
+                for copy in loads(p):
+                    copy.wait()
+            send_plane(c)
 
     total_req = rgroup_v.shape[1]
     groups = rgroup_v[...]
@@ -154,15 +190,23 @@
     len_of = jnp.sum(jnp.where(goes, plen_v[...].astype(F32), 0.0), axis=1, keepdims=True)
     lane = iota((n_seq, HD), 1)
     tab_v[...] = jnp.where(lane == 0, slot_of, len_of).astype(jnp.int32)
-    to_smem = pltpu.make_async_copy(tab_v, tab_s, load_sem.at[blocks + len(others)])
+    to_smem = pltpu.make_async_copy(tab_v, tab_s, load_sem.at[len(pieces) * n_kvh + len(others)])
     to_smem.start()
+    feed(0)
+    for p in range(1, len(pieces)):
+        for copy in loads(p):
+            copy.start()
+    for copy in others:
+        copy.start()
+    for c in range(1, cfg["ahead"]):
+        feed(c)
     to_smem.wait()
 
     for c in range(nc):
-        pltpu.make_async_copy(
-            r1[c].at[pl.ds(0, len(plane) * per_rep)], r1[c].at[pl.ds(0, len(plane) * per_rep)], recv1.at[c]
-        ).wait()
+        came = r1[c].at[pl.ds(0, s1[c].shape[0])]
+        pltpu.make_async_copy(came, came, recv1.at[c]).wait()
         send_line(c)
+        feed(c + cfg["ahead"])
 
     for copy in others:
         copy.wait()
@@ -241,18 +285,12 @@
     keys_blk = n_seq * n_kvh * BLK
     n_at = iota((few, keys_blk), 1)
     n_at = (n_at // BLK) * shard + lax.rem(n_at, BLK)
-    outs = []
     arrived = set()
-    for c, (b, c0, w) in enumerate(chunks):
-        pltpu.make_async_copy(landed_at(c, 0, len(line)), landed_at(c, 0, len(line)), recv2.at[c]).wait()
-        out = pltpu.make_async_copy(
-            landed_at(c, 0, n_seq),
-            land_out.at[:, :, pl.ds(b * BLK, BLK), pl.ds(c0, w)],
-            out_sem.at[c],
-        )
-        out.start()
-        outs.append(out)
-        arrived |= {(b, at) for at in range(c0, c0 + w, HD)}
+    for c, (b, c0, w, steps) in enumerate(chunks):
+        came = landed_at(c, 0, len(line), 0)
+        pltpu.make_async_copy(came, came, recv2.at[c]).wait()
+        if steps in (ALL, (2, 3)):
+            arrived |= {(b, at) for at in range(c0, c0 + w, HD)}
         for h in range(heads):
             k_at, v_at = 2 * h * HD, (2 * h + 1) * HD
             if not {(b, k_at), (b, v_at)} <= arrived:
@@ -277,14 +315,20 @@
         for t in range(STEPS):
             for g in range(gqa):
                 attv[t, :, pl.ds((h * gqa + g) * HD, HD)] = accs[h, pl.ds((t * gqa + g) * rows, rows), :].astype(BF16)
-    out = pltpu.make_async_copy(attv, att_out, out_sem.at[nc])
-    out.start()
-    outs.append(out)
     for c in range(nc):
         pltpu.make_async_copy(s1[c], s1[c], send1.at[c]).wait()
         pltpu.make_async_copy(s2[c], s2[c], send2.at[c]).wait()
-    for out in outs:
-        out.wait()
+
+
+def store(attv, land, att_out, land_out, sem):
+    copies = [pltpu.make_async_copy(attv, att_out, sem.at[0])]
+    parts = land.shape[0] // 4
+    for i in range(parts):
+        copies.append(pltpu.make_async_copy(land.at[pl.ds(i * 4, 4)], land_out.at[pl.ds(i * 4, 4)], sem.at[1 + i]))
+    for copy in copies:
+        copy.start()
+    for copy in copies:
+        copy.wait()
 
 
 def per_device(mesh_shape, prompt_kv, prompt_len, request_group, res_kv, res_len, queries, step_kv):
@@ -296,19 +340,18 @@
     blocks = shard // BLK
     rows, q_cols = queries.shape[1:]
     q_rows = STEPS * rows * (q_cols // (heads * HD))
-    chunks = [(b, c0, 2 * HD) for b in range(blocks) for c0 in range(0, width, 2 * HD)]
+    chunks = CHUNKS
     n_keys = res_kv.shape[0] + 256
-    cfg = dict(mesh=mesh_shape, chunks=chunks, q_tile=128)
-    near, far = n_kvh * n_rep, n_seq
+    cfg = dict(mesh=mesh_shape, chunks=chunks, q_tile=128, ahead=AHEAD)
+    pieces = sorted({chunk[:3] for chunk in chunks})
     v = lambda shape, dtype=BF16: pltpu.VMEM(shape, dtype)
     dma = lambda n: pltpu.SemaphoreType.DMA((n,))
     scratch = (
-        [v((n_req, BLK, all_cols)) for _ in range(blocks)]
-        + [v(((near - 1) * per_rep, BLK, w)) for _, _, w in chunks]
-        + [v((near * per_rep, BLK, w)) for _, _, w in chunks]
-        + [v((far - 1, n_kvh, BLK, w)) for _, _, w in chunks]
+        [v((n_kvh, n_req, BLK, w)) for _, _, w in pieces]
+        + [v(((len(d) * n_rep - (0 in d)) * per_rep, BLK, w)) for _, _, w, d in chunks]
+        + [v((len(d) * n_rep * per_rep, BLK, w)) for _, _, w, d in chunks]
+        + [v((n_seq - 1, len(d), BLK, w)) for _, _, w, d in chunks]
         + [
-            v((n_seq, n_kvh, shard, width)),
             v((heads, n_keys, 2 * HD)),
             v((heads, n_keys, 2 * HD)),
             v((heads, q_rows, 2 * HD)),
@@ -317,25 +360,23 @@
             v((heads, q_rows, HD), F32),
             v((heads, q_rows, HD), F32),
             v((heads, q_rows, HD), F32),
-            v(queries.shape),
             v((n_seq, HD), jnp.int32),
             pltpu.SMEM((n_seq, HD), jnp.int32),
         ]
-        + [dma(blocks + 2 * heads + 3)]
+        + [dma(len(pieces) * n_kvh + 2 * heads + 3)]
         + [dma(len(chunks))] * 4
-        + [dma(len(chunks) + 1)]
     )
     spec = lambda space: pl.BlockSpec(memory_space=space)
-    attention, landed = pl.pallas_call(
+    held = pl.pallas_call(
         functools.partial(kernel, cfg),
         out_shape=(
-            jax.ShapeDtypeStruct(queries.shape, BF16),
-            jax.ShapeDtypeStruct((n_seq, n_kvh, shard, width), BF16),
+            pltpu.VMEM(queries.shape, BF16),
+            pltpu.VMEM((n_seq, n_kvh, shard, width), BF16),
         ),
         in_specs=[spec(s) for s in (pl.ANY, pltpu.SMEM, pltpu.SMEM, pltpu.VMEM, pltpu.VMEM, pl.ANY, pltpu.VMEM, pl.ANY, pl.ANY)],
-        out_specs=(spec(pl.ANY), spec(pl.ANY)),
+        out_specs=(spec(pltpu.VMEM), spec(pltpu.VMEM)),
         scratch_shapes=scratch,
-        compiler_params=pltpu.CompilerParams(collective_id=0, has_side_effects=True, vmem_limit_bytes=56 << 20),
+        compiler_params=pltpu.CompilerParams(collective_id=0, has_side_effects=True, vmem_limit_bytes=58 << 20),
     )(
         prompt_kv,
         prompt_len,
@@ -347,6 +388,14 @@
         queries,
         step_kv,
     )
+    attention, landed = pl.pallas_call(
+        store,
+        out_shape=tuple(jax.ShapeDtypeStruct(a.shape, a.dtype) for a in held),
+        in_specs=[spec(pltpu.VMEM)] * 2,
+        out_specs=(spec(pl.ANY), spec(pl.ANY)),
+        scratch_shapes=[dma(1 + n_seq // 4)],
+        compiler_params=pltpu.CompilerParams(vmem_limit_bytes=2 << 20),
+    )(*held)
     return attention, landed.reshape(n_seq * n_kvh * shard, width)
 
 

time: 97.1 us -> 89 us (0.917)
  local copies, waits for them, and re-layouts: 5.42 us -> 0 us
  Pallas kernels: 90.9 us -> 88.2 us
    unnamed x2 -> x0, local copies, waits for them, and re-layouts: 5.42 us -> none
    pallas_call x1 -> x2, Pallas kernels: 90.9 us -> 88.2 us  [the longest x1 86.4 us: per_device(): pl.pallas_call(functools.partial(kernel, cfg), out_shape=(pltpu.VMEM(quer...]
where the time goes in v2:
time: 89 us; the launch traced here: 88.8 us
  Pallas kernels  88.2 us (99%)
    pallas_call x1, Pallas kernels, per_device(): pl.pallas_call(functools.partial(kernel, cfg), out_shape=(pltpu.VMEM(quer...  86.4 us
    pallas_call x1, Pallas kernels, per_device(): pl.pallas_call(store, out_shape=tuple((jax.ShapeDtypeStruct(a.shape, a.dt...  1.79 us

profile of v2, /device:TPU:1, one launch (start us, length us, event | category | flops | bytes accessed | tf_op | source)
XLA Modules:
  0.0 88.8 jit_solution(18196531685951522512)
XLA Ops:
  0.6 86.4 %shard_map.86 = (bf16[2,32,2048]{2,1,0:T(8,128)(2,1)S(1)}, bf16[16,4,48,512]{3,2,1,0:T(8,128)(2,1)S(1)}) custom-call(bf16[16,48,2048]{2,1,0:T(8,128)(2,1)} %prompt.1, s32[64]{0:T(128)} %plen_s.1, s32[64]{0:T(128)} %rgroup_s.1, s32[1,64]{1,0:T(1,128)} %bitcast.3, s32[1,64]{1,0:T(1,128)} %bitcast.4, bf16[4096,512]{1,0:T(8,128)(2,1)} %res.1, s32[1,31]{1,0:T(1,128)} %rlen.1, ...), custom_call_target="tpu_custom_call" | custom-call | tf_op jit(solution)/shard_map/pallas_call | solution.py:370
  87.0 1.8 %shard_map.87 = (bf16[2,32,2048]{2,1,0:T(8,128)(2,1)}, bf16[16,4,48,512]{3,2,1,0:T(8,128)(2,1)}) custom-call(bf16[2,32,2048]{2,1,0:T(8,128)(2,1)S(1)} %get-tuple-element.6.attv, bf16[16,4,48,512]{3,2,1,0:T(8,128)(2,1)S(1)} %get-tuple-element.7.land), custom_call_target="tpu_custom_call" | custom-call | tf_op jit(solution)/shard_map/pallas_call | solution.py:391

commit v3 on v2

--- a/solution.py
+++ b/solution.py
@@ -17,6 +17,8 @@
 F32 = jnp.float32
 NT = (((1,), (1,)), ((), ()))
 AHEAD = 4
+LAST = 2
+LATE_ORDER = [0, 1, 2, 3, 4, 5, 6, 7]
 ALL = (0, 1, 2, 3)
 CHUNKS = [
     (0, 0, 128, (0,)),
@@ -25,8 +27,19 @@
     (0, 128, 128, ALL),
     (0, 256, 256, ALL),
     (1, 0, 512, ALL),
-    (2, 0, 512, ALL),
+    (2, 0, 256, ALL),
+    (2, 256, 256, ALL),
 ]
+
+
+def packed(values):
+    return sum(v << (3 * i) for i, v in enumerate(values))
+
+
+def nth_plane(p, zed):
+    own = (packed([LATE_ORDER.index(i) for i in range(8)]) >> (3 * zed)) & 7
+    at = p + (p >= own).astype(jnp.int32)
+    return (packed(LATE_ORDER) >> (3 * at)) & 7
 
 
 def wrap(value, size):
@@ -37,7 +50,7 @@
     return lax.broadcasted_iota(jnp.int32, shape, dim)
 
 
-def kernel(cfg, prompt, plen_s, rgroup_s, plen_v, rgroup_v, res, rlen, queries, fresh, attv, land, *scratch):
+def kernel(cfg, prompt, groups_flat, plen, groups_row, res, res_len, queries, fresh, attv, land, *scratch):
     n_seq, n_kvh, n_rep = cfg["mesh"]
     n_z = n_seq // CORES
     n_req, shard, _ = prompt.shape
@@ -58,7 +71,8 @@
     r1 = [next(it) for _ in chunks]
     s2 = [next(it) for _ in chunks]
     kcat, vcat, qcat, qv, fv, accs, sums, maxs, tab_v, tab_s = (next(it) for _ in range(10))
-    load_sem, send1, recv1, send2, recv2 = (next(it) for _ in range(5))
+    rgroup_s, plen_v, rgroup_v, rlen = (next(it) for _ in range(4))
+    load_sem, small_sem, send1, recv1, send2, recv2 = (next(it) for _ in range(6))
 
     seq, kvh, rep = lax.axis_index("seq"), lax.axis_index("kvh"), lax.axis_index("rep")
     zed, core = seq // CORES, lax.rem(seq, CORES)
@@ -90,7 +104,10 @@
             for k in range(n_kvh)
         ]
 
-    for copy in loads(0):
+    small = [(groups_flat, rgroup_s), (groups_row, rgroup_v), (plen, plen_v), (res_len, rlen)]
+    small = [pltpu.make_async_copy(a, b, small_sem.at[i]) for i, (a, b) in enumerate(small)]
+    small[0].start()
+    for copy in loads(0) + small[1:]:
         copy.start()
     others = []
     for h in range(heads):
@@ -106,6 +123,7 @@
     for off in line:
         pl.semaphore_signal(barrier, inc=1, device_id=(line_peer(off), kvh, rep), device_id_type=MESH)
 
+    small[0].wait()
     packed, power = [0] * n_rep, [1] * n_rep
     for q in range(n_req):
         to_rep = lax.rem(rgroup_s[rep * n_req + q], n_rep)
@@ -145,27 +163,36 @@
         b, c0, w, steps = chunks[c]
         return land.at[pl.ds(s, n), pl.ds(k, len(steps)), pl.ds(b * BLK, BLK), pl.ds(c0, w)]
 
+    def line_peers(c):
+        if c < nc - LAST:
+            return [line_peer(off) for off in line]
+        peers = []
+        for p in range(n_z - 1):
+            z_to = nth_plane(p, zed)
+            peers += [z_to * CORES + (p + 1) % 2, z_to * CORES + p % 2]
+        return peers + [line_peer((0, 1))]
+
     def send_line(c):
         b, c0, w, steps = chunks[c]
         first = first_slab(c)
-        for i, off in enumerate(line + [(0, 0)]):
-            s_to = line_peer(off)
+        peers = line_peers(c)
+        for i, s_to in enumerate(peers + [seq]):
             slot, length = jnp.clip(tab_s[s_to, 0], 0, n_rep * per_rep - 1), tab_s[s_to, 1]
             for k in range(len(steps)):
                 piece = r1[c][k * n_rep * per_rep + slot]
                 at = (seq * n_kvh + first + k) * shard + b * BLK + iota((BLK, w), 0)
                 piece = jnp.where(at < length, piece, jnp.zeros_like(piece))
-                if off == (0, 0):
+                if i == len(peers):
                     land[seq, first + k, pl.ds(b * BLK, BLK), pl.ds(c0, w)] = piece
                 else:
                     s2[c][i, k] = piece
-        for i, off in enumerate(line):
+        for i, s_to in enumerate(peers):
             pltpu.make_async_remote_copy(
                 src_ref=s2[c].at[pl.ds(i, 1)],
                 dst_ref=landed_at(c, seq, 1, first),
                 send_sem=send2.at[c],
                 recv_sem=recv2.at[c],
-                device_id=(line_peer(off), kvh, rep),
+                device_id=(s_to, kvh, rep),
                 device_id_type=MESH,
             ).start()
 
@@ -180,6 +207,8 @@
                     copy.wait()
             send_plane(c)
 
+    for copy in small[1:]:
+        copy.wait()
     total_req = rgroup_v.shape[1]
     groups = rgroup_v[...]
     mine = (lax.rem(groups, n_rep) == rep).astype(BF16)
@@ -362,8 +391,12 @@
             v((heads, q_rows, HD), F32),
             v((n_seq, HD), jnp.int32),
             pltpu.SMEM((n_seq, HD), jnp.int32),
+            pltpu.SMEM(request_group.shape, jnp.int32),
+            v((1, request_group.shape[0]), jnp.int32),
+            v((1, request_group.shape[0]), jnp.int32),
+            v(res_len.shape, jnp.int32),
         ]
-        + [dma(len(pieces) * n_kvh + 2 * heads + 3)]
+        + [dma(len(pieces) * n_kvh + 2 * heads + 3), dma(4)]
         + [dma(len(chunks))] * 4
     )
     spec = lambda space: pl.BlockSpec(memory_space=space)
@@ -373,13 +406,12 @@
             pltpu.VMEM(queries.shape, BF16),
             pltpu.VMEM((n_seq, n_kvh, shard, width), BF16),
         ),
-        in_specs=[spec(s) for s in (pl.ANY, pltpu.SMEM, pltpu.SMEM, pltpu.VMEM, pltpu.VMEM, pl.ANY, pltpu.VMEM, pl.ANY, pl.ANY)],
+        in_specs=[spec(pl.ANY)] * 8,
         out_specs=(spec(pltpu.VMEM), spec(pltpu.VMEM)),
         scratch_shapes=scratch,
         compiler_params=pltpu.CompilerParams(collective_id=0, has_side_effects=True, vmem_limit_bytes=58 << 20),
     )(
         prompt_kv,
-        prompt_len,
         request_group,
         prompt_len.reshape(1, -1),
         request_group.reshape(1, -1),

time: 89 us -> 86.2 us (0.969)
  the two profiles are of different devices: /device:TPU:1 before, /device:TPU:64 now
where the time goes in v3:
time: 86.2 us; the launch traced here: 86.1 us
  Pallas kernels  85.5 us (99%)
    pallas_call x1, Pallas kernels, per_device(): pl.pallas_call(functools.partial(kernel, cfg), out_shape=(pltpu.VMEM(quer...  83.7 us
    pallas_call x1, Pallas kernels, per_device(): pl.pallas_call(store, out_shape=tuple((jax.ShapeDtypeStruct(a.shape, a.dt...  1.79 us

profile of v3, /device:TPU:64, one launch (start us, length us, event | category | flops | bytes accessed | tf_op | source)
XLA Modules:
  0.0 86.1 jit_solution(955189780330544319)
XLA Ops:
  0.6 83.7 %shard_map.86 = (bf16[2,32,2048]{2,1,0:T(8,128)(2,1)S(1)}, bf16[16,4,48,512]{3,2,1,0:T(8,128)(2,1)S(1)}) custom-call(bf16[16,48,2048]{2,1,0:T(8,128)(2,1)} %prompt.1, s32[64]{0:T(128)} %groups_flat.1, s32[1,64]{1,0:T(1,128)} %bitcast.4, s32[1,64]{1,0:T(1,128)} %bitcast.3, bf16[4096,512]{1,0:T(8,128)(2,1)} %res.1, s32[1,31]{1,0:T(1,128)} %res_len.1, ...), custom_call_target="tpu_custom_call" | custom-call | tf_op jit(solution)/shard_map/pallas_call | solution.py:403
  84.3 1.8 %shard_map.87 = (bf16[2,32,2048]{2,1,0:T(8,128)(2,1)}, bf16[16,4,48,512]{3,2,1,0:T(8,128)(2,1)}) custom-call(bf16[2,32,2048]{2,1,0:T(8,128)(2,1)S(1)} %get-tuple-element.6.attv, bf16[16,4,48,512]{3,2,1,0:T(8,128)(2,1)S(1)} %get-tuple-element.7.land), custom_call_target="tpu_custom_call" | custom-call | tf_op jit(solution)/shard_map/pallas_call | solution.py:423

commit v4 on v3

--- a/solution.py
+++ b/solution.py
@@ -165,11 +165,11 @@
 
     def line_peers(c):
         if c < nc - LAST:
-            return [line_peer(off) for off in line]
+            steps = [a + core * (b - a) for a, b in zip((4, 3, 2, 1, 5, 6, 7), (4, 5, 6, 7, 3, 2, 1))]
+            return [line_peer((a, b)) for a in steps for b in (0, 1)] + [line_peer((0, 1))]
         peers = []
-        for p in range(n_z - 1):
-            z_to = nth_plane(p, zed)
-            peers += [z_to * CORES + (p + 1) % 2, z_to * CORES + p % 2]
+        for p, half in ((0, 1), (0, 0), (1, 1), (2, 1), (1, 0), (2, 0), (3, 0), (3, 1), (4, 0), (4, 1), (5, 0), (5, 1), (6, 0), (6, 1)):
+            peers.append(nth_plane(p, zed) * CORES + half)
         return peers + [line_peer((0, 1))]
 
     def send_line(c):
@@ -207,6 +207,11 @@
                     copy.wait()
             send_plane(c)
 
+    feed(0)
+    for p in range(1, len(pieces)):
+        for copy in loads(p):
+            copy.start()
+
     for copy in small[1:]:
         copy.wait()
     total_req = rgroup_v.shape[1]
@@ -221,12 +226,6 @@
     tab_v[...] = jnp.where(lane == 0, slot_of, len_of).astype(jnp.int32)
     to_smem = pltpu.make_async_copy(tab_v, tab_s, load_sem.at[len(pieces) * n_kvh + len(others)])
     to_smem.start()
-    feed(0)
-    for p in range(1, len(pieces)):
-        for copy in loads(p):
-            copy.start()
-    for copy in others:
-        copy.start()
     for c in range(1, cfg["ahead"]):
         feed(c)
     to_smem.wait()
@@ -235,6 +234,9 @@
         came = r1[c].at[pl.ds(0, s1[c].shape[0])]
         pltpu.make_async_copy(came, came, recv1.at[c]).wait()
         send_line(c)
+        if c == 0:
+            for copy in others:
+                copy.start()
         feed(c + cfg["ahead"])
 
     for copy in others:

time: 86.2 us -> 86.3 us (level)
  the two profiles are of different devices: /device:TPU:64 before, /device:TPU:32 now
where the time goes in v4:
time: 86.3 us; the launch traced here: 86.2 us
  Pallas kernels  85.5 us (99%)
    pallas_call x1, Pallas kernels, per_device(): pl.pallas_call(functools.partial(kernel, cfg), out_shape=(pltpu.VMEM(quer...  83.7 us
    pallas_call x1, Pallas kernels, per_device(): pl.pallas_call(store, out_shape=tuple((jax.ShapeDtypeStruct(a.shape, a.dt...  1.79 us

profile of v4, /device:TPU:32, one launch (start us, length us, event | category | flops | bytes accessed | tf_op | source)
XLA Modules:
  0.0 86.2 jit_solution(8382151198515540237)
XLA Ops:
  0.6 83.7 %shard_map.86 = (bf16[2,32,2048]{2,1,0:T(8,128)(2,1)S(1)}, bf16[16,4,48,512]{3,2,1,0:T(8,128)(2,1)S(1)}) custom-call(bf16[16,48,2048]{2,1,0:T(8,128)(2,1)} %prompt.1, s32[64]{0:T(128)} %groups_flat.1, s32[1,64]{1,0:T(1,128)} %bitcast.4, s32[1,64]{1,0:T(1,128)} %bitcast.3, bf16[4096,512]{1,0:T(8,128)(2,1)} %res.1, s32[1,31]{1,0:T(1,128)} %res_len.1, ...), custom_call_target="tpu_custom_call" | custom-call | tf_op jit(solution)/shard_map/pallas_call | solution.py:405
  84.4 1.8 %shard_map.87 = (bf16[2,32,2048]{2,1,0:T(8,128)(2,1)}, bf16[16,4,48,512]{3,2,1,0:T(8,128)(2,1)}) custom-call(bf16[2,32,2048]{2,1,0:T(8,128)(2,1)S(1)} %get-tuple-element.6.attv, bf16[16,4,48,512]{3,2,1,0:T(8,128)(2,1)S(1)} %get-tuple-element.7.land), custom_call_target="tpu_custom_call" | custom-call | tf_op jit(solution)/shard_map/pallas_call | solution.py:425
